TPU v7x, 32 devices: a whole 2x2x4 slice. The times are simulated.
32 devices in a mesh: ha: 16 (over z, y, x), ta: 2 (over core).
Axes of the slice: x: 2, y: 2, z: 4, core: 2. Of those that a mesh axis runs over, the one named last changes fastest.
Arguments:
- features: bfloat16 [8, 16, 640, 128], P('ta', 'ha'), may hold values from -6 to 6
- cotangent: bfloat16 [8, 16, 640, 128], P('ta', 'ha'), may hold values from -6 to 6
- kernel: bfloat16 [3, 3, 3, 128, 128], replicated, may hold values from -0.109375 to 0.109375
Outputs:
- grad_features: bfloat16 [8, 16, 640, 128], P('ta', 'ha')
- grad_kernel: float32 [3456, 128], P(('ha', 'ta'))
All inputs are finite; a program needn't handle non-finite values.
Results may differ from a plain program's by a relative error of at most 0.003.
Values may be sent and summed in bfloat16 or wider, within the bound.
A program may use at most 128 MiB of HBM per device.

v0:
```python
import jax
import jax.numpy as jnp
from jax import lax
from jax.sharding import PartitionSpec as P


def passed_along(block, axis, distance):
    devices = range(lax.axis_size(axis))
    route = [(i - distance, i) for i in devices if i - distance in devices]
    return lax.ppermute(block, axis, route)


def with_halo(x, sides, width):
    for axis, dim in sides:
        count, length = (lax.axis_size(axis), x.shape[dim])
        up = [(i, (i + 1) % count) for i in range(count - 1)]
        down = [(j, i) for i, j in up]
        last = lax.slice_in_dim(x, length - width, length, axis=dim)
        leading = lax.slice_in_dim(x, 0, width, axis=dim)
        before = lax.ppermute(last, axis, up)
        after = lax.ppermute(leading, axis, down)
        x = jnp.concatenate([before, x, after], axis=dim)
    return x


def body(features, cotangent, kernel):
    frames, height, breadth, channels = features.shape
    values = features.astype(jnp.float32)
    active = jax.nn.silu(values).astype(jnp.bfloat16)
    future = passed_along(cotangent[:2], "ta", -1)
    cot_ext = jnp.concatenate([cotangent, future], axis=0)
    cot_rows = with_halo(cot_ext, (("ha", 1),), 1)
    cot_pad = jnp.pad(cot_rows, ((0, 0), (0, 0), (1, 1), (0, 0)))
    cot_flat = cotangent.reshape(-1, channels)
    past = passed_along(active[-2:], "ta", 1)
    act_ext = jnp.concatenate([past, active], axis=0)
    act_rows = with_halo(act_ext, (("ha", 1),), 1)
    act_pad = jnp.pad(act_rows, ((0, 0), (0, 0), (1, 1), (0, 0)))
    grad_input = jnp.zeros((frames * height * breadth, channels), jnp.float32)
    blocks = []
    for t_tap in range(3):
        for h_tap in range(3):
            cot_slab = jnp.concatenate(
                [
                    cot_pad[
                        2 - t_tap : 2 - t_tap + frames,
                        2 - h_tap : 2 - h_tap + height,
                        2 - w_tap : 2 - w_tap + breadth,
                    ]
                    for w_tap in range(3)
                ],
                axis=-1,
            ).reshape(-1, 3 * channels)
            stacked = jnp.transpose(kernel[t_tap, h_tap], (0, 2, 1)).reshape(3 * channels, channels)
            grad_input = grad_input + jnp.dot(cot_slab, stacked, preferred_element_type=jnp.float32)
            act_slab = jnp.concatenate(
                [
                    act_pad[t_tap : t_tap + frames, h_tap : h_tap + height, w_tap : w_tap + breadth]
                    for w_tap in range(3)
                ],
                axis=-1,
            ).reshape(-1, 3 * channels)
            blocks.append(
                lax.dot_general(
                    act_slab, cot_flat, (((0,), (0,)), ((), ())), preferred_element_type=jnp.float32
                )
            )
    total_cells = frames * height * breadth * lax.axis_size("ha") * lax.axis_size("ta")
    factor = float(total_cells) ** (-0.5)
    term = jnp.concatenate(blocks, axis=0) * factor
    grad_kernel = lax.psum_scatter(term, ("ha", "ta"), scatter_dimension=0, tiled=True)
    sigmoid_part = jax.nn.sigmoid(values)
    derivative = sigmoid_part * (1.0 + values * (1.0 - sigmoid_part))
    grad_features = (
        cotangent.astype(jnp.float32) + derivative * grad_input.reshape(features.shape)
    ).astype(jnp.bfloat16)
    return (grad_features, grad_kernel)


def solution(mesh):
    placed = (P("ta", "ha", None, None), P("ta", "ha", None, None), P())
    return jax.shard_map(
        body,
        mesh=mesh,
        in_specs=placed,
        out_specs=(P("ta", "ha", None, None), P(("ha", "ta"), None)),
        check_vma=False,
    )
```

profile of v0, /device:TPU:0, one launch (start us, length us, event | category | flops | bytes accessed | tf_op | source)
XLA Modules:
  0.0 224.1 jit_solution(14177028296597618364)
XLA Ops:
  1.6 1.3 collective-permute-start
  5.2 4.9 %collective-permute-start.1 = (bf16[6,1,640,128]{3,2,1,0:T(8,128)(2,1)S(1)}, bf16[6,1,640,128]{3,2,1,0:T(8,128)(2,1)S(1)}, u32[]{:S(2)}, u32[]{:S(2)}) collective-permute-start(bf16[6,1,640,128]{3,2,1,0:T(8,128)(2,1)S(1)} %constant_dynamic-update-slice_fusion), channel_id=1, source_target_pairs={{0,2},{2,4},{4,6},{6,8},{8,10},{10,12},{12,14},{14,16},{16,18},{18... | collective-permute-start | bytes 2949128 | tf_op jit(solution)/shard_map/ppermute | solution.py:20
  10.1 1.3 collective-permute-start.2
  11.4 2.2 copy.22
  13.6 2.0 fusion.110
  16.6 1.6 copy.36
  18.3 1.6 copy.37
  19.9 1.6 copy.38
  21.6 1.6 copy.39
  25.0 2.2 copy.23
  27.3 25.1 %collective-permute-done.1 = bf16[6,1,640,128]{3,2,1,0:T(8,128)(2,1)S(1)} collective-permute-done((bf16[6,1,640,128]{3,2,1,0:T(8,128)(2,1)S(1)}, bf16[6,1,640,128]{3,2,1,0:T(8,128)(2,1)S(1)}, u32[]{:S(2)}, u32[]{:S(2)}) %collective-permute-start.1) | collective-permute-done | bytes 983072 | tf_op jit(solution)/shard_map/ppermute | solution.py:20
  52.4 1.9 collective-permute-done.2
  55.4 3.3 %fusion.104 = (bf16[4,1,640,128]{3,2,1,0:T(8,128)(2,1)S(1)}, bf16[4,1,640,128]{3,2,1,0:T(8,128)(2,1)S(1)}, bf16[4,1,640,128]{3,2,1,0:T(8,128)(2,1)S(1)}, bf16[4,...) fusion(bf16[6,3,642,128]{3,2,1,0:T(8,128)(2,1)S(1)} %fusion.10), kind=kLoop, calls=%fused_computation.147 | loop fusion | bytes 23592960 | tf_op jit(solution)/shard_map/slice | solution.py:45
  69.6 1.8 convolution_add_fusion
  71.3 1.8 copy.33
  73.1 2.5 %fusion.64 = (bf16[4,1,640,128]{2,3,0,1:T(8,128)(2,1)S(1)}, bf16[4,1,640,128]{2,3,0,1:T(8,128)(2,1)}) fusion(bf16[4,1,640,128]{2,3,0,1:T(8,128)(2,1)} %copy.23, f32[4,1,640,128]{2,3,0,1:T(8,128)S(1)} %copy.33, bf16[4,1,640,128]{2,3,0,1:T(8,128)(2,1)S(1)} %copy-done.1), kind=kLoop, calls=%fused_computation.101 | loop fusion | flops 4587520 | bytes 3932160 | tf_op jit(solution)/shard_map/convert_element_type | solution.py:29
  75.7 1.3 collective-permute-start.3
  78.4 3.5 %collective-permute-start.4 = (bf16[6,1,640,128]{2,3,0,1:T(8,128)(2,1)S(1)}, bf16[6,1,640,128]{2,3,0,1:T(8,128)(2,1)S(1)}, u32[]{:S(2)}, u32[]{:S(2)}) collective-permute-start(bf16[6,1,640,128]{2,3,0,1:T(8,128)(2,1)S(1)} %pad_maximum_fusion.9), channel_id=1, source_target_pairs={{0,2},{2,4},{4,6},{6,8},{8,10},{10,12},{12,14},{14,16},{16,18},{18... | collective-permute-start | bytes 2949128 | tf_op jit(solution)/shard_map/ppermute | solution.py:20
  81.8 1.5 collective-permute-start.5
  83.5 40.9 %collective-permute-done.4 = bf16[6,1,640,128]{2,3,0,1:T(8,128)(2,1)S(1)} collective-permute-done((bf16[6,1,640,128]{2,3,0,1:T(8,128)(2,1)S(1)}, bf16[6,1,640,128]{2,3,0,1:T(8,128)(2,1)S(1)}, u32[]{:S(2)}, u32[]{:S(2)}) %collective-permute-start.4) | collective-permute-done | bytes 983072 | tf_op jit(solution)/shard_map/ppermute | solution.py:20
  125.1 3.0 %select_maximum_fusion = bf16[6,3,642,128]{2,3,0,1:T(8,128)(2,1)S(1)} fusion(bf16[6,1,640,128]{2,3,0,1:T(8,128)(2,1)S(1)} %collective-permute-done.5, bf16[6,1,640,128]{2,3,0,1:T(8,128)(2,1)S(1)} %collective-permute-done.4, bf16[4,1,640,128]{2,3,0,1:T(8,128)(2,1)S(1)} %get-tuple-element.69, bf16[2,1,640,128]{2,3,0,1:T(8,128)(2,1)S(1)} %collective-permute-done.3), kind=kLoop, calls=%fused_computation.14 | loop fusion | flops 22187520 | bytes 5907456 | tf_op jit(solution)/shard_map/concatenate | solution.py:22
  128.1 4.0 %fusion.103 = (bf16[4,1,640,128]{2,3,0,1:T(8,128)(2,1)S(1)}, bf16[4,1,640,128]{2,3,0,1:T(8,128)(2,1)S(1)}, bf16[4,1,640,128]{2,3,0,1:T(8,128)(2,1)S(1)}, bf16[4,...) fusion(bf16[6,3,642,128]{2,3,0,1:T(8,128)(2,1)S(1)} %select_max, ...), kind=kLoop, calls=%fused_computation.146 | loop fusion | bytes 23592960 | tf_op jit(solution)/shard_map/slice | solution.py:58
  138.8 80.3 %fusion = f32[112,128]{1,0:T(8,128)S(1)} fusion(f32[3456,128]{1,0:T(8,128)S(1)} %broadcast_multiply_fusion), kind=kCustom, calls=%all-reduce-scatter | all-reduce-scatter fusion | flops 458753 | bytes 1826816
  219.1 1.3 collective-permute-start.6
  (68 shorter events, 30.5 us)
Async XLA Ops:
  1.6 3.5 %collective-permute-start = (bf16[2,1,640,128]{3,2,1,0:T(8,128)(2,1)S(1)}, bf16[2,1,640,128]{3,2,1,0:T(8,128)(2,1)S(1)}, u32[]{:S(2)}, u32[]{:S(2)}) collective-permute-start(bf16[2,1,640,128]{3,2,1,0:T(8,128)(2,1)S(1)} %slice.227), channel_id=1, source_target_pairs={{1,0},{3,2},{5,4},{7,6},{9,8},{11,10},{13,12},{15,14},{17,16},{19,... | collective-permute-start | bytes 983048 | tf_op jit(solution)/shard_map/ppermute | solution.py:10
  5.2 47.2 %collective-permute-start.1 = (bf16[6,1,640,128]{3,2,1,0:T(8,128)(2,1)S(1)}, bf16[6,1,640,128]{3,2,1,0:T(8,128)(2,1)S(1)}, u32[]{:S(2)}, u32[]{:S(2)}) collective-permute-start(bf16[6,1,640,128]{3,2,1,0:T(8,128)(2,1)S(1)} %constant_dynamic-update-slice_fusion), channel_id=1, source_target_pairs={{0,2},{2,4},{4,6},{6,8},{8,10},{10,12},{12,14},{14,16},{16,18},{18... | collective-permute-start | bytes 2949128 | tf_op jit(solution)/shard_map/ppermute | solution.py:20
  10.1 44.2 %collective-permute-start.2 = (bf16[6,1,640,128]{3,2,1,0:T(8,128)(2,1)S(1)}, bf16[6,1,640,128]{3,2,1,0:T(8,128)(2,1)S(1)}, u32[]{:S(2)}, u32[]{:S(2)}) collective-permute-start(bf16[6,1,640,128]{3,2,1,0:T(8,128)(2,1)S(1)} %constant_dynamic-update-slice_fusion), channel_id=1, source_target_pairs={{2,0},{4,2},{6,4},{8,6},{10,8},{12,10},{14,12},{16,14},{18,16},{20... | collective-permute-start | bytes 2949128 | tf_op jit(solution)/shard_map/ppermute | solution.py:21
  59.7 0.9 copy-start.8
  61.6 0.9 copy-start.7
  62.5 0.9 copy-start.6
  64.1 0.9 copy-start.5
  65.0 0.9 copy-start.4
  65.9 1.1 copy-start
  67.0 0.9 copy-start.3
  71.3 1.8 copy-start.1
  75.7 2.5 %collective-permute-start.3 = (bf16[2,1,640,128]{2,3,0,1:T(8,128)(2,1)S(1)}, bf16[2,1,640,128]{2,3,0,1:T(8,128)(2,1)S(1)}, u32[]{:S(2)}, u32[]{:S(2)}) collective-permute-start(bf16[2,1,640,128]{2,3,0,1:T(8,128)(2,1)S(1)} %slice.316), channel_id=1, source_target_pairs={{0,1},{2,3},{4,5},{6,7},{8,9},{10,11},{12,13},{14,15},{16,17},{18,... | collective-permute-start | bytes 983048 | tf_op jit(solution)/shard_map/ppermute | solution.py:10
  78.4 46.0 %collective-permute-start.4 = (bf16[6,1,640,128]{2,3,0,1:T(8,128)(2,1)S(1)}, bf16[6,1,640,128]{2,3,0,1:T(8,128)(2,1)S(1)}, u32[]{:S(2)}, u32[]{:S(2)}) collective-permute-start(bf16[6,1,640,128]{2,3,0,1:T(8,128)(2,1)S(1)} %pad_maximum_fusion.9), channel_id=1, source_target_pairs={{0,2},{2,4},{4,6},{6,8},{8,10},{10,12},{12,14},{14,16},{16,18},{18... | collective-permute-start | bytes 2949128 | tf_op jit(solution)/shard_map/ppermute | solution.py:20
  81.8 43.3 %collective-permute-start.5 = (bf16[6,1,640,128]{2,3,0,1:T(8,128)(2,1)S(1)}, bf16[6,1,640,128]{2,3,0,1:T(8,128)(2,1)S(1)}, u32[]{:S(2)}, u32[]{:S(2)}) collective-permute-start(bf16[6,1,640,128]{2,3,0,1:T(8,128)(2,1)S(1)} %pad_maximum_fusion.9), channel_id=1, source_target_pairs={{2,0},{4,2},{6,4},{8,6},{10,8},{12,10},{14,12},{16,14},{18,16},{20... | collective-permute-start | bytes 2949128 | tf_op jit(solution)/shard_map/ppermute | solution.py:21
  138.7 83.1 %copy-start.2 = (bf16[4,1,640,128]{2,3,0,1:T(8,128)(2,1)S(1)}, bf16[4,1,640,128]{2,3,0,1:T(8,128)(2,1)}, u32[]{:S(2)}) copy-start(bf16[4,1,640,128]{2,3,0,1:T(8,128)(2,1)} %get-tuple-element.70) | copy-start | bytes 1966084
  219.1 4.0 %collective-permute-start.6 = (f32[112,128]{1,0:T(8,128)S(1)}, f32[112,128]{1,0:T(8,128)S(1)}, u32[]{:S(2)}, u32[]{:S(2)}) collective-permute-start(f32[112,128]{1,0:T(8,128)S(1)} %fusion), channel_id=1, source_target_pairs={{0,1},{1,2},{2,3},{3,4},{4,5},{5,6},{6,7},{7,8},{8,9},{9,10},{10,1... | collective-permute-start | bytes 172040
  220.4 2.6 %collective-permute-start.7 = (f32[12,128]{1,0:T(8,128)S(1)}, f32[12,128]{1,0:T(8,128)S(1)}, u32[]{:S(2)}, u32[]{:S(2)}) collective-permute-start(f32[12,128]{1,0:T(8,128)S(1)} %slice.345), channel_id=1, source_target_pairs={{0,2},{1,3},{2,4},{3,5},{4,6},{5,7},{6,8},{7,9},{8,10},{9,11},{10,... | collective-permute-start | bytes 18440
where the time goes:
time: 225 us; the launch traced here: 224 us
  blocking collectives  80.3 us (36%)
  waiting for transfers between devices  71.2 us (32%)
  local copies, waits for them, and re-layouts  32.2 us (14%)
  starting transfers between devices  16.3 us (7%)
  matrix products  13.4 us (6%)
  other arithmetic  9.51 us (4%)
    unnamed x1, blocking collectives  80.3 us
    ppermute x2, waiting for transfers between devices, with_halo(): before = lax.ppermute(last, axis, up)  66 us
    unnamed x34, local copies, waits for them, and re-layouts  18.8 us
    ppermute x2, starting transfers between devices, with_halo(): before = lax.ppermute(last, axis, up)  8.38 us
    dot_general x9, matrix products, body(): jnp.dot(cot_slab, stacked, preferred_element_type=jnp.float32)  7.36 us
    dot_general x9, matrix products, body(): lax.dot_general(act_slab, cot_flat, (((0,), (0,)), ((), ())), preferred_e...  6.09 us
  transfers between devices with their start and end apart: 8, of which 7 were waited for; matrix products, arithmetic and copies ran while one was open for 8% of the time, Pallas kernels for 0%

commit v1 on v0

v1 whole, which is shorter than its diff:
```python
import jax
import jax.numpy as jnp
from jax import lax
from jax.sharding import PartitionSpec as P


def passed_along(block, axis, distance):
    devices = range(lax.axis_size(axis))
    route = [(i - distance, i) for i in devices if i - distance in devices]
    return lax.ppermute(block, axis, route)


def halo_rows(x, axis):
    count = lax.axis_size(axis)
    up = [(i, i + 1) for i in range(count - 1)]
    down = [(j, i) for i, j in up]
    return lax.ppermute(x, axis, up), lax.ppermute(x, axis, down)


def body(features, cotangent, kernel):
    frames, height, breadth, channels = features.shape
    values = features.astype(jnp.float32)
    active = jax.nn.silu(values).astype(jnp.bfloat16)
    act_flat = active.reshape(-1, channels)
    before, after = halo_rows(cotangent[:, -1:], "ha") if height == 1 else (
        lax.ppermute(cotangent[:, -1:], "ha", [(i, i + 1) for i in range(lax.axis_size("ha") - 1)]),
        lax.ppermute(cotangent[:, :1], "ha", [(i + 1, i) for i in range(lax.axis_size("ha") - 1)]),
    )
    cot_rows = jnp.concatenate([before, cotangent, after], axis=1)
    future = passed_along(cot_rows[:2], "ta", -1)
    cot_ext = jnp.concatenate([cot_rows, future], axis=0)
    cot_pad = jnp.pad(cot_ext, ((0, 0), (0, 0), (1, 1), (0, 0)))
    grad_input = jnp.zeros((frames * height * breadth, channels), jnp.float32)
    blocks = []
    for t_tap in range(3):
        for h_tap in range(3):
            cot_slab = jnp.concatenate(
                [
                    cot_pad[
                        2 - t_tap : 2 - t_tap + frames,
                        2 - h_tap : 2 - h_tap + height,
                        2 - w_tap : 2 - w_tap + breadth,
                    ]
                    for w_tap in range(3)
                ],
                axis=-1,
            ).reshape(-1, 3 * channels)
            stacked = jnp.transpose(kernel[t_tap, h_tap], (0, 2, 1)).reshape(3 * channels, channels)
            grad_input = grad_input + jnp.dot(cot_slab, stacked, preferred_element_type=jnp.float32)
            part = lax.dot_general(
                act_flat, cot_slab, (((0,), (0,)), ((), ())), preferred_element_type=jnp.float32
            )
            blocks += [part[:, k * channels : (k + 1) * channels] for k in range(3)]
    rows, cores = lax.axis_size("ha"), lax.axis_size("ta")
    total_cells = frames * height * breadth * rows * cores
    factor = float(total_cells) ** (-0.5)
    term = (jnp.concatenate(blocks, axis=0) * factor).reshape(rows, cores, -1, channels)
    mine = lax.axis_index("ta")
    kept = lax.dynamic_index_in_dim(term, mine, 1, keepdims=False)
    given = lax.dynamic_index_in_dim(term, 1 - mine, 1, keepdims=False)
    kept = kept + lax.ppermute(given, "ta", [(0, 1), (1, 0)])
    got = lax.all_to_all(kept.astype(jnp.bfloat16), "ha", 0, 0, tiled=True)
    grad_kernel = jnp.sum(got.astype(jnp.float32), axis=0)
    sigmoid_part = jax.nn.sigmoid(values)
    derivative = sigmoid_part * (1.0 + values * (1.0 - sigmoid_part))
    grad_features = (
        cotangent.astype(jnp.float32) + derivative * grad_input.reshape(features.shape)
    ).astype(jnp.bfloat16)
    return (grad_features, grad_kernel)


def solution(mesh):
    placed = (P("ta", "ha", None, None), P("ta", "ha", None, None), P())
    return jax.shard_map(
        body,
        mesh=mesh,
        in_specs=placed,
        out_specs=(P("ta", "ha", None, None), P(("ha", "ta"), None)),
        check_vma=False,
    )
```

time: 225 us -> 109 us (0.48)
  blocking collectives: 80.3 us -> 0 us
  waiting for transfers between devices: 71.2 us -> 38.5 us
  local copies, waits for them, and re-layouts: 32.2 us -> 26 us
  other arithmetic: 9.51 us -> 15.1 us
    unnamed x1 -> x0, blocking collectives: 80.3 us -> none
    ppermute x4 -> x3, waiting for transfers between devices: 68.7 us -> 28.2 us  [the longest x2 28.2 us: halo_rows(): return (lax.ppermute(x, axis, up), lax.ppermute(x, axis, down))]
    all_to_all x0 -> x1, waiting for transfers between devices: none -> 10.3 us  [body(): got = lax.all_to_all(kept.astype(jnp.bfloat16), 'ha', 0, 0, tiled=True)]
    all_to_all x0 -> x1, starting transfers between devices: none -> 5.89 us  [body(): got = lax.all_to_all(kept.astype(jnp.bfloat16), 'ha', 0, 0, tiled=True)]
    slice x5 -> x0, local copies, waits for them, and re-layouts: 5.4 us -> none  [the longest x3 4.37 us: body(): act_pad[t_tap:t_tap + frames, h_tap:h_tap + height, w_tap:w_tap + breadth]]
    concatenate x5, other arithmetic: 2.51 us -> 7.86 us  [body(): jnp.concatenate([cot_pad[2 - t_tap:2 - t_tap + frames, 2 - h_tap:2 - h_ta...]
    unnamed x34 -> x93, local copies, waits for them, and re-layouts: 18.8 us -> 14.5 us
    ppermute x4 -> x3, starting transfers between devices: 11.1 us -> 8.06 us  [the longest x2 6.81 us: halo_rows(): return (lax.ppermute(x, axis, up), lax.ppermute(x, axis, down))]
  transfers between devices with their start and end apart: 8 -> 5, of which waited for: 7 -> 3; matrix products, arithmetic and copies ran while one was open for 8% -> 18% of each run, Pallas kernels for 0% -> 0%
where the time goes in v1:
time: 109 us; the launch traced here: 108 us
  waiting for transfers between devices  38.5 us (35%)
  local copies, waits for them, and re-layouts  26 us (24%)
  starting transfers between devices  15.4 us (14%)
  other arithmetic  15.1 us (14%)
  matrix products  11.5 us (11%)
  between operations  1.34 us (1%)
    ppermute x2, waiting for transfers between devices, halo_rows(): return (lax.ppermute(x, axis, up), lax.ppermute(x, axis, down))  28.2 us
    unnamed x93, local copies, waits for them, and re-layouts  14.5 us
    all_to_all x1, waiting for transfers between devices, body(): got = lax.all_to_all(kept.astype(jnp.bfloat16), 'ha', 0, 0, tiled=True)  10.3 us
    concatenate x5, other arithmetic, body(): jnp.concatenate([cot_pad[2 - t_tap:2 - t_tap + frames, 2 - h_tap:2 - h_ta...  7.86 us
    ppermute x2, starting transfers between devices, halo_rows(): return (lax.ppermute(x, axis, up), lax.ppermute(x, axis, down))  6.81 us
    dot_general x9, matrix products, body(): jnp.dot(cot_slab, stacked, preferred_element_type=jnp.float32)  6.3 us
    all_to_all x1, starting transfers between devices, body(): got = lax.all_to_all(kept.astype(jnp.bfloat16), 'ha', 0, 0, tiled=True)  5.89 us
    dot_general x9, matrix products, body(): lax.dot_general(act_flat, cot_slab, (((0,), (0,)), ((), ())), preferred_e...  5.21 us
  transfers between devices with their start and end apart: 5, of which 3 were waited for; matrix products, arithmetic and copies ran while one was open for 18% of the time, Pallas kernels for 0%

profile of v1, /device:TPU:0, one launch (start us, length us, event | category | flops | bytes accessed | tf_op | source)
XLA Modules:
  0.0 107.9 jit_solution(11892491484990673367)
XLA Ops:
  0.6 1.3 %collective-permute-start.1 = (bf16[4,1,640,128]{3,2,0,1:T(8,128)(2,1)}, bf16[4,1,640,128]{3,2,0,1:T(8,128)(2,1)S(1)}, u32[]{:S(2)}, u32[]{:S(2)}) collective-permute-start(bf16[4,1,640,128]{3,2,0,1:T(8,128)(2,1)} %bitcast.160), channel_id=1, source_target_pairs={{2,0},{4,2},{6,4},{8,6},{10,8},{12,10},{14,12},{16,14},{18,16},{20... | collective-permute-start | bytes 1966088 | tf_op jit(solution)/shard_map/ppermute | solution.py:17
  1.9 5.5 %collective-permute-start = (bf16[4,1,640,128]{3,2,0,1:T(8,128)(2,1)}, bf16[4,1,640,128]{3,2,0,1:T(8,128)(2,1)S(1)}, u32[]{:S(2)}, u32[]{:S(2)}) collective-permute-start(bf16[4,1,640,128]{3,2,0,1:T(8,128)(2,1)} %bitcast.161), channel_id=1, source_target_pairs={{0,2},{2,4},{4,6},{6,8},{8,10},{10,12},{12,14},{14,16},{16,18},{18... | collective-permute-start | bytes 1966088 | tf_op jit(solution)/shard_map/ppermute | solution.py:17
  7.5 13.8 %collective-permute-done.1 = bf16[4,1,640,128]{3,2,0,1:T(8,128)(2,1)S(1)} collective-permute-done((bf16[4,1,640,128]{3,2,0,1:T(8,128)(2,1)}, bf16[4,1,640,128]{3,2,0,1:T(8,128)(2,1)S(1)}, u32[]{:S(2)}, u32[]{:S(2)}) %collective-permute-start.1) | collective-permute-done | bytes 655392 | tf_op jit(solution)/shard_map/ppermute | solution.py:17
  21.2 14.4 %collective-permute-done = bf16[4,1,640,128]{3,2,0,1:T(8,128)(2,1)S(1)} collective-permute-done((bf16[4,1,640,128]{3,2,0,1:T(8,128)(2,1)}, bf16[4,1,640,128]{3,2,0,1:T(8,128)(2,1)S(1)}, u32[]{:S(2)}, u32[]{:S(2)}) %collective-permute-start) | collective-permute-done | bytes 655392 | tf_op jit(solution)/shard_map/ppermute | solution.py:17
  35.7 2.0 %pad_maximum_fusion.10 = bf16[2,3,640,128]{3,2,0,1:T(8,128)(2,1)} fusion(bf16[4,1,640,128]{3,2,0,1:T(8,128)(2,1)S(1)} %collective-permute-done.1, bf16[4,1,640,128]{3,2,0,1:T(8,128)(2,1)} %bitcast.162, bf16[4,1,640,128]{3,2,0,1:T(8,128)(2,1)S(1)} %collective-permute-done), kind=kLoop, calls=%fused_computation.57 | loop fusion | flops 983040 | bytes 2949120 | tf_op jit(solution)/shard_map/concatenate | solution.py:29
  37.7 1.4 %collective-permute-start.2 = (bf16[2,3,640,128]{3,2,0,1:T(8,128)(2,1)}, bf16[2,3,640,128]{3,2,0,1:T(8,128)(2,1)S(1)}, u32[]{:S(2)}, u32[]{:S(2)}) collective-permute-start(bf16[2,3,640,128]{3,2,0,1:T(8,128)(2,1)} %pad_maximum_fusion.10), channel_id=1, source_target_pairs={{1,0},{3,2},{5,4},{7,6},{9,8},{11,10},{13,12},{15,14},{17,16},{19,... | collective-permute-start | bytes 2949128 | tf_op jit(solution)/shard_map/ppermute | solution.py:10
  39.1 2.0 %fusion.66 = (bf16[1,1,3,128,128]{4,3,2,1,0:T(8,128)(2,1)}, bf16[1,1,3,128,128]{4,3,2,1,0:T(8,128)(2,1)}, bf16[1,1,3,128,128]{4,3,2,1,0:T(8,128)(2,1)}, bf16[1,1...) fusion(bf16[3,3,3,128,128]{4,3,2,1,0:T(8,128)(2,1)} %param.5), kind=kLoop, calls=%fused_computation.113 | loop fusion | bytes 1769472 | tf_op jit(solution)/shard_map/slice | solution.py:48
  41.1 1.6 %copy.133 = bf16[1,1,3,128,128]{3,4,2,1,0:T(8,128)(2,1)} copy(bf16[1,1,3,128,128]{4,3,2,1,0:T(8,128)(2,1)} %get-tuple-element.28) | data formatting | bytes 196608
  42.7 1.6 %copy.132 = bf16[1,1,3,128,128]{3,4,2,1,0:T(8,128)(2,1)} copy(bf16[1,1,3,128,128]{4,3,2,1,0:T(8,128)(2,1)} %get-tuple-element.29) | data formatting | bytes 196608
  44.4 1.6 %copy.131 = bf16[1,1,3,128,128]{3,4,2,1,0:T(8,128)(2,1)} copy(bf16[1,1,3,128,128]{4,3,2,1,0:T(8,128)(2,1)} %get-tuple-element.30) | data formatting | bytes 196608
  50.0 1.9 %pad_slice_fusion.1 = (bf16[4,1,640,128]{3,2,0,1:T(8,128)(2,1)S(1)}, bf16[4,1,640,128]{3,2,0,1:T(8,128)(2,1)S(1)}, bf16[4,1,640,128]{3,2,0,1:T(8,128)(2,1)S(1)},...) fusion(bf16[6,3,640,128]{3,2,0,1:T(8,128)(2,1)S(1)} %pad_maximu, ...), kind=kLoop, calls=%fused_computation.95 | loop fusion | bytes 10158080 | tf_op jit(solution)/shard_map/slice | solution.py:39
  53.1 1.6 %pad_maximum_fusion.1 = (bf16[4,1,640,384]{3,2,0,1:T(8,128)(2,1)}, bf16[4,1,640,384]{3,2,0,1:T(8,128)(2,1)S(1)}) fusion(bf16[4,1,640,128]{3,2,0,1:T(8,128)(2,1)S(1)} %get-tuple-element.3, bf16[4,1,640,128]{3,2,0,1:T(8,128)(2,1)S(1)} %get-tuple-element.24, bf16[4,1,640,128]{3,2,0,1:T(8,128)(2,1)S(1)} %get-tuple-element.25, ...), kind=kLoop, calls=%fused_computation.9 | loop fusion | flops 11796480 | bytes 7864320 | tf_op jit(solution)/shard_map/concatenate | solution.py:37
  54.7 1.8 %pad_slice_fusion = (bf16[4,1,640,128]{3,2,0,1:T(8,128)(2,1)S(1)}, bf16[4,1,640,128]{3,2,0,1:T(8,128)(2,1)S(1)}, bf16[4,1,640,128]{3,2,0,1:T(8,128)(2,1)S(1)}, b...) fusion(bf16[6,3,640,128]{3,2,0,1:T(8,128)(2,1)S(1)} %pad_maximu, ...), kind=kLoop, calls=%fused_computation.94 | loop fusion | bytes 12124160 | tf_op jit(solution)/shard_map/slice | solution.py:39
  57.7 2.1 %pad_maximum_fusion.5 = (bf16[4,1,640,384]{3,2,0,1:T(8,128)(2,1)}, bf16[4,1,640,384]{3,2,0,1:T(8,128)(2,1)}) fusion(bf16[4,1,640,128]{3,2,0,1:T(8,128)(2,1)S(1)} %get-tuple-element.13, bf16[4,1,640,128]{3,2,0,1:T(8,128)(2,1)S(1)} %get-tuple-element.20, bf16[4,1,640,128]{3,2,0,1:T(8,128)(2,1)S(1)} %get-tuple-element.10, ...), kind=kLoop, calls=%fused_computation.13 | loop fusion | flops 11796480 | bytes 7864320 | tf_op jit(solution)/shard_map/concatenate | solution.py:37
  61.0 2.2 %pad_maximum_fusion.3 = (bf16[4,1,640,384]{3,2,0,1:T(8,128)(2,1)}, bf16[4,1,640,384]{3,2,0,1:T(8,128)(2,1)}) fusion(bf16[4,1,640,128]{3,2,0,1:T(8,128)(2,1)S(1)} %get-tuple-element.7, bf16[4,1,640,128]{3,2,0,1:T(8,128)(2,1)S(1)} %get-tuple-element.22, bf16[4,1,640,128]{3,2,0,1:T(8,128)(2,1)S(1)} %get-tuple-element.6, ...), kind=kLoop, calls=%fused_computation.11 | loop fusion | flops 11796480 | bytes 7864320 | tf_op jit(solution)/shard_map/concatenate | solution.py:37
  66.3 1.4 %broadcast_multiply_fusion = f32[3456,128]{1,0:T(8,128)} fusion(f32[3456,128]{1,0:T(8,128)S(1)} %slice_dynamic-update-slice_fusion), kind=kLoop, calls=%fused_computation.63 | loop fusion | flops 442368 | bytes 3538944 | tf_op jit(solution)/shard_map/mul | solution.py:57
  67.7 2.6 %mul.29 = f32[16,2,108,128]{3,2,1,0:T(8,128)} reshape(f32[3456,128]{1,0:T(8,128)} %broadcast_multiply_fusion) | data formatting | bytes 3538944 | tf_op jit(solution)/shard_map/mul | solution.py:57
  70.3 1.7 %constant_dynamic-slice_fusion.1 = (f32[16,1,108,128]{3,2,1,0:T(8,128)S(1)}, f32[16,1,108,128]{3,2,1,0:T(8,128)S(1)}) fusion(f32[16,2,108,128]{3,2,1,0:T(8,128)} %mul.29, s32[]{:T(128)S(6)} %select_n.7, s32[]{:T(128)S(6)} %select_n.8), kind=kLoop, calls=%fused_computation.93 | loop fusion | bytes 3538952 | tf_op jit(solution)/shard_map/jit(dynamic_index_in_dim)/dynamic_slice | solution.py:59
  72.3 1.2 %collective-permute-start.3 = (f32[16,108,128]{2,0,1:T(8,128)S(1)}, f32[16,108,128]{2,0,1:T(8,128)S(1)}, u32[]{:S(2)}, u32[]{:S(2)}) collective-permute-start(f32[16,108,128]{2,0,1:T(8,128)S(1)} %bitcast.176), channel_id=1, source_target_pairs={{0,1},{1,0},{2,3},{3,2},{4,5},{5,4},{6,7},{7,6},{8,9},{9,8},{10,11... | collective-permute-start | bytes 2654216 | tf_op jit(solution)/shard_map/ppermute | solution.py:61
  86.1 5.9 %all-to-all-start = ((bf16[16,108,128]{2,1,0:T(8,128)(2,1)}), bf16[16,108,128]{2,1,0:T(8,128)(2,1)}, u32[]{:S(2)}, u32[]{:S(2)}) async-start(bf16[16,108,128]{2,1,0:T(8,128)(2,1)} %copy.115), calls=%async_computation | async-start | bytes 917504 | tf_op jit(solution)/shard_map/all_to_all | solution.py:62
  92.0 1.4 %pad_maximum_fusion.9 = bf16[4,1,640,384]{3,2,0,1:T(8,128)(2,1)S(1)} fusion(bf16[4,1,640,128]{3,2,0,1:T(8,128)(2,1)} %copy-done.11, bf16[4,1,640,128]{3,2,0,1:T(8,128)(2,1)S(1)} %collective-permute-done, bf16[4,1,640,128]{3,2,0,1:T(8,128)(2,1)S(1)} %copy-done.10), kind=kLoop, calls=%fused_computation.17 | loop fusion | flops 5898240 | bytes 3932160 | tf_op jit(solution)/shard_map/concatenate | solution.py:37
  94.5 1.4 %fusion.25 = bf16[4,1,640,128]{3,2,1,0:T(8,128)(2,1)} fusion(f32[4,1,640,128]{3,2,1,0:T(8,128)S(1)} %bitcast.175, bf16[4,1,640,128]{3,2,1,0:T(8,128)(2,1)S(1)} %copy-done.21, bf16[4,1,640,128]{3,2,1,0:T(8,128)(2,1)S(1)} %copy-done), kind=kLoop, calls=%fused_computation.46 | loop fusion | flops 3932160 | bytes 3276800 | tf_op jit(solution)/shard_map/convert_element_type | solution.py:68
  95.9 10.3 %all-to-all-done = bf16[16,108,128]{2,1,0:T(8,128)(2,1)} async-done(((bf16[16,108,128]{2,1,0:T(8,128)(2,1)}), bf16[16,108,128]{2,1,0:T(8,128)(2,1)}, u32[]{:S(2)}, u32[]{:S(2)}) %all-to-all-start) | async-done | bytes 442400 | tf_op jit(solution)/shard_map/all_to_all | solution.py:62
  106.2 1.7 %convert_reduce_fusion = f32[108,128]{1,0:T(8,128)} fusion(bf16[16,108,128]{2,1,0:T(8,128)(2,1)} %all-to-all-done), kind=kLoop, calls=%fused_computation.59 | loop fusion | flops 428544 | bytes 497664 | tf_op jit(solution)/shard_map/reduce_sum | solution.py:63
  (117 shorter events, 23.9 us)
Async XLA Ops:
  0.6 20.6 %collective-permute-start.1 = (bf16[4,1,640,128]{3,2,0,1:T(8,128)(2,1)}, bf16[4,1,640,128]{3,2,0,1:T(8,128)(2,1)S(1)}, u32[]{:S(2)}, u32[]{:S(2)}) collective-permute-start(bf16[4,1,640,128]{3,2,0,1:T(8,128)(2,1)} %bitcast.160), channel_id=1, source_target_pairs={{2,0},{4,2},{6,4},{8,6},{10,8},{12,10},{14,12},{16,14},{18,16},{20... | collective-permute-start | bytes 1966088 | tf_op jit(solution)/shard_map/ppermute | solution.py:17
  1.9 33.7 %collective-permute-start = (bf16[4,1,640,128]{3,2,0,1:T(8,128)(2,1)}, bf16[4,1,640,128]{3,2,0,1:T(8,128)(2,1)S(1)}, u32[]{:S(2)}, u32[]{:S(2)}) collective-permute-start(bf16[4,1,640,128]{3,2,0,1:T(8,128)(2,1)} %bitcast.161), channel_id=1, source_target_pairs={{0,2},{2,4},{4,6},{6,8},{8,10},{10,12},{12,14},{14,16},{16,18},{18... | collective-permute-start | bytes 1966088 | tf_op jit(solution)/shard_map/ppermute | solution.py:17
  21.2 28.0 %copy-start.6 = (bf16[4,1,640,128]{3,2,0,1:T(8,128)(2,1)}, bf16[4,1,640,128]{3,2,0,1:T(8,128)(2,1)S(1)}, u32[]{:S(2)}) copy-start(bf16[4,1,640,128]{3,2,0,1:T(8,128)(2,1)S(1)} %collective-permute-done.1) | copy-start | bytes 1966084
  37.7 11.6 %copy-start = (bf16[4,1,640,128]{3,2,1,0:T(8,128)(2,1)S(1)}, bf16[4,1,640,128]{3,2,1,0:T(8,128)(2,1)}, u32[]{:S(2)}) copy-start(bf16[4,1,640,128]{3,2,1,0:T(8,128)(2,1)} %param.4) | copy-start | bytes 1966084
  37.7 11.5 %collective-permute-start.2 = (bf16[2,3,640,128]{3,2,0,1:T(8,128)(2,1)}, bf16[2,3,640,128]{3,2,0,1:T(8,128)(2,1)S(1)}, u32[]{:S(2)}, u32[]{:S(2)}) collective-permute-start(bf16[2,3,640,128]{3,2,0,1:T(8,128)(2,1)} %pad_maximum_fusion.10), channel_id=1, source_target_pairs={{1,0},{3,2},{5,4},{7,6},{9,8},{11,10},{13,12},{15,14},{17,16},{19,... | collective-permute-start | bytes 2949128 | tf_op jit(solution)/shard_map/ppermute | solution.py:10
  50.0 2.0 %copy-start.20 = (bf16[4,1,640,128]{3,2,1,0:T(8,128)(2,1)S(1)}, bf16[4,1,640,128]{3,2,1,0:T(8,128)(2,1)}, u32[]{:S(2)}) copy-start(bf16[4,1,640,128]{3,2,1,0:T(8,128)(2,1)} %param.3) | copy-start | bytes 1966084
  52.0 13.7 %copy-start.9 = (bf16[4,1,640,128]{3,2,0,1:T(8,128)(2,1)}, bf16[4,1,640,128]{3,2,0,1:T(8,128)(2,1)S(1)}, u32[]{:S(2)}) copy-start(bf16[4,1,640,128]{3,2,0,1:T(8,128)(2,1)S(1)} %get-tuple-element.2) | copy-start | bytes 1966084
  56.5 7.0 %copy-start.12 = (bf16[4,1,640,128]{3,2,0,1:T(8,128)(2,1)}, bf16[4,1,640,128]{3,2,0,1:T(8,128)(2,1)S(1)}, u32[]{:S(2)}) copy-start(bf16[4,1,640,128]{3,2,0,1:T(8,128)(2,1)S(1)} %get-tuple-element.16) | copy-start | bytes 1966084
  56.5 7.0 %copy-start.14 = (bf16[4,1,640,128]{3,2,0,1:T(8,128)(2,1)}, bf16[4,1,640,128]{3,2,0,1:T(8,128)(2,1)S(1)}, u32[]{:S(2)}) copy-start(bf16[4,1,640,128]{3,2,0,1:T(8,128)(2,1)S(1)} %get-tuple-element.17) | copy-start | bytes 1966084
  56.5 8.4 %copy-start.16 = (bf16[4,1,640,128]{3,2,0,1:T(8,128)(2,1)}, bf16[4,1,640,128]{3,2,0,1:T(8,128)(2,1)S(1)}, u32[]{:S(2)}) copy-start(bf16[4,1,640,128]{3,2,0,1:T(8,128)(2,1)S(1)} %get-tuple-element.18) | copy-start | bytes 1966084
  56.6 8.4 %copy-start.18 = (bf16[4,1,640,128]{3,2,0,1:T(8,128)(2,1)}, bf16[4,1,640,128]{3,2,0,1:T(8,128)(2,1)S(1)}, u32[]{:S(2)}) copy-start(bf16[4,1,640,128]{3,2,0,1:T(8,128)(2,1)S(1)} %get-tuple-element.19) | copy-start | bytes 1966084
  56.6 9.1 %copy-start.11 = (bf16[4,1,640,128]{3,2,0,1:T(8,128)(2,1)}, bf16[4,1,640,128]{3,2,0,1:T(8,128)(2,1)S(1)}, u32[]{:S(2)}) copy-start(bf16[4,1,640,128]{3,2,0,1:T(8,128)(2,1)S(1)} %get-tuple-element.12) | copy-start | bytes 1966084
  70.3 3.3 %copy-start.1 = (bf16[4,1,640,384]{3,2,0,1:T(8,128)(2,1)S(1)}, bf16[4,1,640,384]{3,2,0,1:T(8,128)(2,1)}, u32[]{:S(2)}) copy-start(bf16[4,1,640,384]{3,2,0,1:T(8,128)(2,1)} %get-tuple-element.37) | copy-start | bytes 5898244
  72.3 1.9 %copy-start.28 = (bf16[1,1,3,128,128]{3,4,2,1,0:T(8,128)(2,1)S(1)}, bf16[1,1,3,128,128]{3,4,2,1,0:T(8,128)(2,1)}, u32[]{:S(2)}) copy-start(bf16[1,1,3,128,128]{3,4,2,1,0:T(8,128)(2,1)} %copy.126) | copy-start | bytes 294916
  72.3 12.5 %collective-permute-start.3 = (f32[16,108,128]{2,0,1:T(8,128)S(1)}, f32[16,108,128]{2,0,1:T(8,128)S(1)}, u32[]{:S(2)}, u32[]{:S(2)}) collective-permute-start(f32[16,108,128]{2,0,1:T(8,128)S(1)} %bitcast.176), channel_id=1, source_target_pairs={{0,1},{1,0},{2,3},{3,2},{4,5},{5,4},{6,7},{7,6},{8,9},{9,8},{10,11... | collective-permute-start | bytes 2654216 | tf_op jit(solution)/shard_map/ppermute | solution.py:61
  74.3 1.5 %copy-start.5 = (bf16[4,1,640,384]{3,2,0,1:T(8,128)(2,1)S(1)}, bf16[4,1,640,384]{3,2,0,1:T(8,128)(2,1)}, u32[]{:S(2)}) copy-start(bf16[4,1,640,384]{3,2,0,1:T(8,128)(2,1)} %get-tuple-element.39) | copy-start | bytes 5898244
  75.8 1.5 %copy-start.4 = (bf16[4,1,640,384]{3,2,0,1:T(8,128)(2,1)S(1)}, bf16[4,1,640,384]{3,2,0,1:T(8,128)(2,1)}, u32[]{:S(2)}) copy-start(bf16[4,1,640,384]{3,2,0,1:T(8,128)(2,1)} %get-tuple-element.40) | copy-start | bytes 5898244
  75.8 1.5 %copy-start.26 = (bf16[1,1,3,128,128]{3,4,2,1,0:T(8,128)(2,1)S(1)}, bf16[1,1,3,128,128]{3,4,2,1,0:T(8,128)(2,1)}, u32[]{:S(2)}) copy-start(bf16[1,1,3,128,128]{3,4,2,1,0:T(8,128)(2,1)} %copy.128) | copy-start | bytes 294916
  77.4 1.5 %copy-start.3 = (bf16[4,1,640,384]{3,2,0,1:T(8,128)(2,1)S(1)}, bf16[4,1,640,384]{3,2,0,1:T(8,128)(2,1)}, u32[]{:S(2)}) copy-start(bf16[4,1,640,384]{3,2,0,1:T(8,128)(2,1)} %get-tuple-element.41) | copy-start | bytes 5898244
  78.9 1.5 %copy-start.25 = (bf16[1,1,3,128,128]{3,4,2,1,0:T(8,128)(2,1)S(1)}, bf16[1,1,3,128,128]{3,4,2,1,0:T(8,128)(2,1)}, u32[]{:S(2)}) copy-start(bf16[1,1,3,128,128]{3,4,2,1,0:T(8,128)(2,1)} %copy.130) | copy-start | bytes 294916
  80.5 1.7 %copy-start.17 = (bf16[4,1,640,128]{3,2,0,1:T(8,128)(2,1)S(1)}, bf16[4,1,640,128]{3,2,0,1:T(8,128)(2,1)}, u32[]{:S(2)}) copy-start(bf16[4,1,640,128]{3,2,0,1:T(8,128)(2,1)} %copy-done.16) | copy-start | bytes 1966084
  80.5 1.9 %copy-start.19 = (bf16[4,1,640,128]{3,2,0,1:T(8,128)(2,1)S(1)}, bf16[4,1,640,128]{3,2,0,1:T(8,128)(2,1)}, u32[]{:S(2)}) copy-start(bf16[4,1,640,128]{3,2,0,1:T(8,128)(2,1)} %copy-done.18) | copy-start | bytes 1966084
  84.8 7.1 %copy-start.10 = (bf16[4,1,640,128]{3,2,0,1:T(8,128)(2,1)S(1)}, bf16[4,1,640,128]{3,2,0,1:T(8,128)(2,1)}, u32[]{:S(2)}) copy-start(bf16[4,1,640,128]{3,2,0,1:T(8,128)(2,1)} %copy-done.9) | copy-start | bytes 1966084
  86.1 20.1 %all-to-all-start = ((bf16[16,108,128]{2,1,0:T(8,128)(2,1)}), bf16[16,108,128]{2,1,0:T(8,128)(2,1)}, u32[]{:S(2)}, u32[]{:S(2)}) async-start(bf16[16,108,128]{2,1,0:T(8,128)(2,1)} %copy.115), calls=%async_computation | async-start | bytes 917504 | tf_op jit(solution)/shard_map/all_to_all | solution.py:62
  (10 other events, 12.3 us)

commit v2 on v1

v2 whole, which is shorter than its diff:
```python
import functools

import jax
import jax.numpy as jnp
from jax import lax
from jax.experimental import pallas as pl
from jax.experimental.pallas import tpu as pltpu
from jax.sharding import PartitionSpec as P

MESH = pl.DeviceIdType.MESH
LEAD = 8
CHUNKS = 4


def fused(
    rows, cores, factor,
    feat, cot, kern, grad_features, grad_kernel,
    ext, future, acts, padded, partial, acc, give, got, out, landed,
    halo_send, halo_recv, future_send, future_recv, pass_send, pass_recv,
    pair_send, pair_recv, spread_send, spread_recv,
):
    frames, breadth, channels = feat.shape
    wide = 3 * channels
    share, tall = grad_kernel.shape[0], give.shape[1]
    ha, ta = lax.axis_index("ha"), lax.axis_index("ta")
    mate = 1 - ta

    barrier = pltpu.get_barrier_semaphore()

    def greet(s, _):
        pl.semaphore_signal(barrier, inc=1, device_id=(lax.rem(ha + s, rows), ta), device_id_type=MESH)
        return 0

    lax.fori_loop(1, rows, greet, 0)
    pl.semaphore_signal(barrier, inc=1, device_id=(ha, mate), device_id_type=MESH)
    pl.semaphore_wait(barrier, rows)

    def halo(side, frame):
        return pltpu.make_async_remote_copy(
            src_ref=cot.at[frame],
            dst_ref=ext.at[side, frame],
            send_sem=halo_send.at[side, frame],
            recv_sem=halo_recv.at[side, frame],
            device_id=(ha + 1 if side == 0 else ha - 1, ta),
            device_id_type=MESH,
        )

    def ahead(frame):
        return pltpu.make_async_remote_copy(
            src_ref=cot.at[frame],
            dst_ref=future.at[frame],
            send_sem=future_send.at[frame],
            recv_sem=future_recv.at[frame],
            device_id=(ha, mate),
            device_id_type=MESH,
        )

    def relay(side, frame):
        return pltpu.make_async_remote_copy(
            src_ref=ext.at[side, frame],
            dst_ref=ext.at[side, frames + frame],
            send_sem=pass_send.at[side, frame],
            recv_sem=pass_recv.at[side, frame],
            device_id=(ha, mate),
            device_id_type=MESH,
        )

    sends = (ha < rows - 1, ha > 0)
    takes = (ha > 0, ha < rows - 1)

    for frame in range(frames):
        for side in range(2):
            @pl.when(sends[side])
            def _():
                halo(side, frame).start()

    @pl.when(ta == 1)
    def _():
        for frame in range(2):
            ahead(frame).start()

    for side in range(2):
        @pl.when(jnp.logical_not(takes[side]))
        def _():
            ext[side, :frames] = jnp.zeros((frames, breadth, channels), ext.dtype)

    edge = jnp.zeros((LEAD, channels), jnp.float32)
    padded[:LEAD] = edge
    padded[LEAD + breadth :] = edge
    acc[...] = jnp.zeros_like(acc)

    def activate(t, _):
        v = feat[t].astype(jnp.float32)
        active = v / (1.0 + jnp.exp(-v))
        padded[LEAD : LEAD + breadth] = active
        for k in range(3):
            acts[t, :, k * channels : (k + 1) * channels] = padded[
                LEAD - 1 + k : LEAD - 1 + k + breadth
            ].astype(jnp.bfloat16)
        partial[t] = jnp.zeros(partial.shape[1:], jnp.float32)
        return 0

    lax.fori_loop(0, frames, activate, 0)

    nt = (((1,), (1,)), ((), ()))
    tn = (((0,), (0,)), ((), ()))

    def span(e):
        return max(0, e - 2), min(frames, e + 1)

    def middle(e, source):
        def step(t, _):
            i = t - e + 2
            block = source[...]
            tap = i * 3 + 1
            partial[t, LEAD : LEAD + breadth] += lax.dot_general(
                block, kern[tap], nt, preferred_element_type=jnp.float32
            )
            start = pl.multiple_of(tap * wide, wide)
            acc[pl.ds(start, wide)] += lax.dot_general(
                acts[t], block, tn, preferred_element_type=jnp.float32
            )
            return 0

        lax.fori_loop(*span(e), step, 0)

    def outer(e):
        def step(t, _):
            i = t - e + 2
            block = jnp.concatenate([ext[0, e], ext[1, e]], axis=1)
            weights = jnp.concatenate([kern[i * 3 + 2], kern[i * 3]], axis=1)
            partial[t, LEAD : LEAD + breadth] += lax.dot_general(
                block, weights, nt, preferred_element_type=jnp.float32
            )
            both = lax.dot_general(acts[t], block, tn, preferred_element_type=jnp.float32)
            low = pl.multiple_of((i * 3 + 2) * wide, wide)
            high = pl.multiple_of(i * 3 * wide, wide)
            acc[pl.ds(low, wide)] += both[:, :channels]
            acc[pl.ds(high, wide)] += both[:, channels:]
            return 0

        lax.fori_loop(*span(e), step, 0)

    for e in range(frames):
        middle(e, cot.at[e])

    @pl.when(ta == 0)
    def _():
        for frame in range(2):
            ahead(frame).wait_recv()
            middle(frames + frame, future.at[frame])

    for e in range(frames):
        for side in range(2):
            @pl.when(takes[side])
            def _():
                halo(side, e).wait_recv()

        if e < 2:
            @pl.when(ta == 1)
            def _():
                for side in range(2):
                    relay(side, e).start()

        if e == frames - 1:
            @pl.when(ta == 0)
            def _():
                for frame in range(2):
                    for side in range(2):
                        relay(side, frame).wait_recv()
                    outer(frames + frame)

        outer(e)

    per = rows // CHUNKS

    def pair(chunk):
        part = pl.ds(chunk * per, per)
        return pltpu.make_async_remote_copy(
            src_ref=give.at[part],
            dst_ref=got.at[part],
            send_sem=pair_send.at[chunk],
            recv_sem=pair_recv.at[chunk],
            device_id=(ha, mate),
            device_id_type=MESH,
        )

    def spread(h, slot):
        return pltpu.make_async_remote_copy(
            src_ref=out.at[h],
            dst_ref=landed.at[slot],
            send_sem=spread_send.at[h],
            recv_sem=spread_recv.at[slot],
            device_id=(h, ta),
            device_id_type=MESH,
        )

    for chunk in range(CHUNKS):
        def pick(h, _):
            give[h] = acc[pl.ds((cores * h + mate) * share, tall)]
            return 0

        lax.fori_loop(chunk * per, (chunk + 1) * per, pick, 0)
        pair(chunk).start()

    for chunk in range(CHUNKS):
        pair(chunk).wait_recv()

    def scatter(s, _):
        h = lax.rem(ha + s, rows)
        mine = acc[pl.ds((cores * h + ta) * share, tall)] + got[h]
        out[h] = mine.astype(out.dtype)
        spread(h, ha).start()
        return 0

    lax.fori_loop(1, rows, scatter, 0)

    def finish(t, _):
        summed = (
            partial[t, LEAD + 1 : LEAD + 1 + breadth, :channels]
            + partial[t, LEAD : LEAD + breadth, channels : 2 * channels]
            + partial[t, LEAD - 1 : LEAD - 1 + breadth, 2 * channels :]
        )
        v = feat[t].astype(jnp.float32)
        s = 1.0 / (1.0 + jnp.exp(-v))
        slope = s * (1.0 + v * (1.0 - s))
        grad_features[t] = (cot[t].astype(jnp.float32) + slope * summed).astype(grad_features.dtype)
        return 0

    lax.fori_loop(0, frames, finish, 0)

    total = acc[pl.ds((cores * ha + ta) * share, tall)] + got[ha]

    def collect(s, total):
        h = lax.rem(ha + rows - s, rows)
        spread(h, h).wait_recv()
        return total + landed[h].astype(jnp.float32)

    total = lax.fori_loop(1, rows, collect, total)
    grad_kernel[...] = total[:share] * factor

    def drain(s, _):
        h = lax.rem(ha + s, rows)
        spread(h, ha).wait_send()
        return 0

    lax.fori_loop(1, rows, drain, 0)
    for chunk in range(CHUNKS):
        pair(chunk).wait_send()
    for frame in range(frames):
        for side in range(2):
            @pl.when(sends[side])
            def _():
                halo(side, frame).wait_send()

    @pl.when(ta == 1)
    def _():
        for frame in range(2):
            ahead(frame).wait_send()
            for side in range(2):
                relay(side, frame).wait_send()


def body(features, cotangent, kernel):
    frames, height, breadth, channels = features.shape
    rows, cores = lax.axis_size("ha"), lax.axis_size("ta")
    taps = kernel.shape[0] * kernel.shape[1] * kernel.shape[2]
    wide = 3 * channels
    share = taps * channels // (rows * cores)
    tall = -(-share // 16) * 16
    factor = float(frames * height * breadth * rows * cores) ** (-0.5)
    vmem = pl.BlockSpec(memory_space=pltpu.VMEM)
    dma = pltpu.SemaphoreType.DMA
    grad_features, grad_kernel = pl.pallas_call(
        functools.partial(fused, rows, cores, factor),
        out_shape=(
            jax.ShapeDtypeStruct((frames, breadth, channels), jnp.bfloat16),
            jax.ShapeDtypeStruct((share, channels), jnp.float32),
        ),
        in_specs=[vmem] * 3,
        out_specs=(vmem, vmem),
        scratch_shapes=[
            pltpu.VMEM((2, frames + 2, breadth, channels), jnp.bfloat16),
            pltpu.VMEM((2, breadth, channels), jnp.bfloat16),
            pltpu.VMEM((frames, breadth, wide), jnp.bfloat16),
            pltpu.VMEM((breadth + 2 * LEAD, channels), jnp.float32),
            pltpu.VMEM((frames, breadth + 2 * LEAD, wide), jnp.float32),
            pltpu.VMEM((taps * channels + 16, channels), jnp.float32),
            pltpu.VMEM((rows, tall, channels), jnp.float32),
            pltpu.VMEM((rows, tall, channels), jnp.float32),
            pltpu.VMEM((rows, tall, channels), jnp.bfloat16),
            pltpu.VMEM((rows, tall, channels), jnp.bfloat16),
            dma((2, frames)), dma((2, frames)), dma((2,)), dma((2,)), dma((2, 2)), dma((2, 2)),
            dma((CHUNKS,)), dma((CHUNKS,)), dma((rows,)), dma((rows,)),
        ],
        compiler_params=pltpu.CompilerParams(
            collective_id=0, has_side_effects=True, vmem_limit_bytes=48 * 1024 * 1024
        ),
        cost_estimate=pl.CostEstimate(
            flops=4 * frames * breadth * taps * channels * channels,
            bytes_accessed=6 * frames * breadth * channels + 2 * taps * channels * channels,
            transcendentals=2 * frames * breadth * channels,
        ),
    )(
        features.reshape(frames, breadth, channels),
        cotangent.reshape(frames, breadth, channels),
        kernel.reshape(9, wide, channels),
    )
    return (grad_features.reshape(features.shape), grad_kernel)


def solution(mesh):
    placed = (P("ta", "ha", None, None), P("ta", "ha", None, None), P())
    return jax.shard_map(
        body,
        mesh=mesh,
        in_specs=placed,
        out_specs=(P("ta", "ha", None, None), P(("ha", "ta"), None)),
        check_vma=False,
    )
```

time: 109 us -> 55.9 us (0.51)
  the two profiles are of different devices: /device:TPU:0 before, /device:TPU:29 now
where the time goes in v2:
time: 55.9 us; the launch traced here: 55.6 us
  Pallas kernels  50.2 us (90%)
  local copies, waits for them, and re-layouts  4.8 us (9%)
  between operations  0.65 us (1%)
    pallas_call x1, Pallas kernels, body(): pl.pallas_call(functools.partial(fused, rows, cores, factor), out_shape=(...  50.2 us
    unnamed x8, local copies, waits for them, and re-layouts  4.8 us

profile of v2, /device:TPU:29, one launch (start us, length us, event | category | flops | bytes accessed | tf_op | source)
XLA Modules:
  0.0 55.6 jit_solution(358320272385702004)
XLA Ops:
  0.6 0.0 copy-start
  0.6 1.2 %copy-done = bf16[3,3,3,128,128]{4,3,2,1,0:T(8,128)(2,1)S(1)} copy-done((bf16[3,3,3,128,128]{4,3,2,1,0:T(8,128)(2,1)S(1)}, bf16[3,3,3,128,128]{4,3,2,1,0:T(8,128)(2,1)}, u32[]{:S(2)}) %copy-start) | copy-done | bytes 884760
  1.8 0.0 copy-start.1
  1.8 1.1 %copy-done.1 = bf16[4,1,640,128]{3,2,1,0:T(8,128)(2,1)S(1)} copy-done((bf16[4,1,640,128]{3,2,1,0:T(8,128)(2,1)S(1)}, bf16[4,1,640,128]{3,2,1,0:T(8,128)(2,1)}, u32[]{:S(2)}) %copy-start.1) | copy-done | bytes 655384
  2.9 0.0 copy-start.2
  2.9 1.1 %copy-done.2 = bf16[4,1,640,128]{3,2,1,0:T(8,128)(2,1)S(1)} copy-done((bf16[4,1,640,128]{3,2,1,0:T(8,128)(2,1)S(1)}, bf16[4,1,640,128]{3,2,1,0:T(8,128)(2,1)}, u32[]{:S(2)}) %copy-start.2) | copy-done | bytes 655384
  4.0 50.2 %shard_map.50 = (bf16[4,640,128]{2,1,0:T(8,128)(2,1)S(1)}, f32[108,128]{1,0:T(8,128)S(1)}) custom-call(bf16[4,640,128]{2,1,0:T(8,128)(2,1)S(1)} %bitcast.8, bf16[4,640,128]{2,1,0:T(8,128)(2,1)S(1)} %bitcast.9, bf16[9,384,128]{2,1,0:T(8,128)(2,1)S(1)} %bitcast.7), custom_call_target="tpu_custom_call" | custom-call | flops 4529848320 | bytes 2850816 | tf_op jit(solution)/shard_map/pallas_call | solution.py:274
  54.2 0.8 %copy.8 = bf16[4,1,640,128]{3,2,1,0:T(8,128)(2,1)} copy(bf16[4,1,640,128]{3,2,1,0:T(8,128)(2,1)S(1)} %bitcast.6) | data formatting | bytes 1310720
  55.0 0.6 %copy.9 = f32[108,128]{1,0:T(8,128)} copy(f32[108,128]{1,0:T(8,128)S(1)} %get-tuple-element.11) | data formatting | bytes 110592
Async XLA Ops:
  0.6 1.2 %copy-start = (bf16[3,3,3,128,128]{4,3,2,1,0:T(8,128)(2,1)S(1)}, bf16[3,3,3,128,128]{4,3,2,1,0:T(8,128)(2,1)}, u32[]{:S(2)}) copy-start(bf16[3,3,3,128,128]{4,3,2,1,0:T(8,128)(2,1)} %param.5) | copy-start | bytes 2654212
  1.8 1.1 %copy-start.1 = (bf16[4,1,640,128]{3,2,1,0:T(8,128)(2,1)S(1)}, bf16[4,1,640,128]{3,2,1,0:T(8,128)(2,1)}, u32[]{:S(2)}) copy-start(bf16[4,1,640,128]{3,2,1,0:T(8,128)(2,1)} %param.3) | copy-start | bytes 1966084
  2.9 1.1 %copy-start.2 = (bf16[4,1,640,128]{3,2,1,0:T(8,128)(2,1)S(1)}, bf16[4,1,640,128]{3,2,1,0:T(8,128)(2,1)}, u32[]{:S(2)}) copy-start(bf16[4,1,640,128]{3,2,1,0:T(8,128)(2,1)} %param.4) | copy-start | bytes 1966084

commit v3 on v2

--- a/solution.py
+++ b/solution.py
@@ -14,9 +14,9 @@
 
 def fused(
     rows, cores, factor,
-    feat, cot, kern, grad_features, grad_kernel,
-    ext, future, acts, padded, partial, acc, give, got, out, landed,
-    halo_send, halo_recv, future_send, future_recv, pass_send, pass_recv,
+    feat_hbm, cot_hbm, kern_hbm, grad_features, grad_kernel,
+    feat, cot, kern, load_sem, ext, future, acts, padded, partial, acc, give, got, out, landed,
+    near_send, near_recv, far_send, far_recv, future_send, future_recv, pass_send, pass_recv,
     pair_send, pair_recv, spread_send, spread_recv,
 ):
     frames, breadth, channels = feat.shape
@@ -25,6 +25,13 @@
     ha, ta = lax.axis_index("ha"), lax.axis_index("ta")
     mate = 1 - ta
 
+    loads = [
+        pltpu.make_async_copy(source, target, load_sem.at[slot])
+        for slot, (source, target) in enumerate(((feat_hbm, feat), (cot_hbm, cot), (kern_hbm, kern)))
+    ]
+    for load in loads:
+        load.start()
+
     barrier = pltpu.get_barrier_semaphore()
 
     def greet(s, _):
@@ -35,19 +42,32 @@
     pl.semaphore_signal(barrier, inc=1, device_id=(ha, mate), device_id_type=MESH)
     pl.semaphore_wait(barrier, rows)
 
-    def halo(side, frame):
-        return pltpu.make_async_remote_copy(
-            src_ref=cot.at[frame],
+    odd = lax.rem(ha, 2)
+    near_side, far_side = 1 - odd, odd
+
+    def near(frame, side):
+        return pltpu.make_async_remote_copy(
+            src_ref=cot_hbm.at[frame],
             dst_ref=ext.at[side, frame],
-            send_sem=halo_send.at[side, frame],
-            recv_sem=halo_recv.at[side, frame],
-            device_id=(ha + 1 if side == 0 else ha - 1, ta),
+            send_sem=near_send.at[frame],
+            recv_sem=near_recv.at[frame],
+            device_id=(ha + 1 - 2 * odd, ta),
+            device_id_type=MESH,
+        )
+
+    def far(frame):
+        return pltpu.make_async_remote_copy(
+            src_ref=ext.at[near_side, frame],
+            dst_ref=ext.at[far_side, frame],
+            send_sem=far_send.at[frame],
+            recv_sem=far_recv.at[frame],
+            device_id=(ha + 2 - 4 * odd, ta),
             device_id_type=MESH,
         )
 
     def ahead(frame):
         return pltpu.make_async_remote_copy(
-            src_ref=cot.at[frame],
+            src_ref=cot_hbm.at[frame],
             dst_ref=future.at[frame],
             send_sem=future_send.at[frame],
             recv_sem=future_recv.at[frame],
@@ -55,39 +75,38 @@
             device_id_type=MESH,
         )
 
-    def relay(side, frame):
+    def relay(side, kind, frame):
         return pltpu.make_async_remote_copy(
             src_ref=ext.at[side, frame],
             dst_ref=ext.at[side, frames + frame],
-            send_sem=pass_send.at[side, frame],
-            recv_sem=pass_recv.at[side, frame],
+            send_sem=pass_send.at[kind, frame],
+            recv_sem=pass_recv.at[kind, frame],
             device_id=(ha, mate),
             device_id_type=MESH,
         )
 
-    sends = (ha < rows - 1, ha > 0)
-    takes = (ha > 0, ha < rows - 1)
+    first, last = ha < 2, ha >= rows - 2
+    even = odd == 0
+    hands_on = jnp.logical_not(jnp.logical_or(jnp.logical_and(even, last), jnp.logical_and(odd == 1, first)))
+    takes = jnp.logical_not(jnp.logical_or(jnp.logical_and(even, first), jnp.logical_and(odd == 1, last)))
 
     for frame in range(frames):
-        for side in range(2):
-            @pl.when(sends[side])
-            def _():
-                halo(side, frame).start()
+        near(frame, far_side).start()
 
     @pl.when(ta == 1)
     def _():
         for frame in range(2):
             ahead(frame).start()
 
-    for side in range(2):
-        @pl.when(jnp.logical_not(takes[side]))
-        def _():
-            ext[side, :frames] = jnp.zeros((frames, breadth, channels), ext.dtype)
+    @pl.when(jnp.logical_not(takes))
+    def _():
+        ext[far_side, :frames] = jnp.zeros((frames, breadth, channels), ext.dtype)
 
     edge = jnp.zeros((LEAD, channels), jnp.float32)
     padded[:LEAD] = edge
     padded[LEAD + breadth :] = edge
     acc[...] = jnp.zeros_like(acc)
+    loads[0].wait()
 
     def activate(t, _):
         v = feat[t].astype(jnp.float32)
@@ -124,7 +143,20 @@
 
         lax.fori_loop(*span(e), step, 0)
 
-    def outer(e):
+    def outer_kernel(e):
+        def step(t, _):
+            i = t - e + 2
+            block = jnp.concatenate([ext[0, e], ext[1, e]], axis=1)
+            both = lax.dot_general(acts[t], block, tn, preferred_element_type=jnp.float32)
+            low = pl.multiple_of((i * 3 + 2) * wide, wide)
+            high = pl.multiple_of(i * 3 * wide, wide)
+            acc[pl.ds(low, wide)] += both[:, :channels]
+            acc[pl.ds(high, wide)] += both[:, channels:]
+            return 0
+
+        lax.fori_loop(*span(e), step, 0)
+
+    def outer_input(e):
         def step(t, _):
             i = t - e + 2
             block = jnp.concatenate([ext[0, e], ext[1, e]], axis=1)
@@ -132,45 +164,65 @@
             partial[t, LEAD : LEAD + breadth] += lax.dot_general(
                 block, weights, nt, preferred_element_type=jnp.float32
             )
-            both = lax.dot_general(acts[t], block, tn, preferred_element_type=jnp.float32)
-            low = pl.multiple_of((i * 3 + 2) * wide, wide)
-            high = pl.multiple_of(i * 3 * wide, wide)
-            acc[pl.ds(low, wide)] += both[:, :channels]
-            acc[pl.ds(high, wide)] += both[:, channels:]
             return 0
 
         lax.fori_loop(*span(e), step, 0)
 
-    for e in range(frames):
-        middle(e, cot.at[e])
-
-    @pl.when(ta == 0)
-    def _():
-        for frame in range(2):
-            ahead(frame).wait_recv()
-            middle(frames + frame, future.at[frame])
-
-    for e in range(frames):
-        for side in range(2):
-            @pl.when(takes[side])
-            def _():
-                halo(side, e).wait_recv()
+    def hand_on(e):
+        near(e, near_side).wait_recv()
+
+        @pl.when(hands_on)
+        def _():
+            far(e).start()
 
         if e < 2:
             @pl.when(ta == 1)
             def _():
-                for side in range(2):
-                    relay(side, e).start()
-
-        if e == frames - 1:
-            @pl.when(ta == 0)
+                relay(near_side, 0, e).start()
+
+    def arrive(e):
+        @pl.when(takes)
+        def _():
+            far(e).wait_recv()
+
+        if e < 2:
+            @pl.when(ta == 1)
             def _():
-                for frame in range(2):
-                    for side in range(2):
-                        relay(side, frame).wait_recv()
-                    outer(frames + frame)
-
-        outer(e)
+                relay(far_side, 1, e).start()
+
+    loads[1].wait()
+    loads[2].wait()
+    hand_on(0)
+    middle(0, cot.at[0])
+    middle(1, cot.at[1])
+    hand_on(1)
+    middle(2, cot.at[2])
+    hand_on(2)
+    arrive(0)
+    outer_kernel(0)
+    middle(3, cot.at[3])
+    hand_on(3)
+    arrive(1)
+    outer_kernel(1)
+
+    @pl.when(ta == 0)
+    def _():
+        for frame in range(2):
+            ahead(frame).wait_recv()
+            middle(frames + frame, future.at[frame])
+
+    arrive(2)
+    outer_kernel(2)
+
+    @pl.when(ta == 0)
+    def _():
+        for frame in range(2):
+            relay(near_side, 0, frame).wait_recv()
+            relay(far_side, 1, frame).wait_recv()
+            outer_kernel(frames + frame)
+
+    arrive(3)
+    outer_kernel(3)
 
     per = rows // CHUNKS
 
@@ -195,25 +247,38 @@
             device_id_type=MESH,
         )
 
-    for chunk in range(CHUNKS):
-        def pick(h, _):
-            give[h] = acc[pl.ds((cores * h + mate) * share, tall)]
-            return 0
-
-        lax.fori_loop(chunk * per, (chunk + 1) * per, pick, 0)
+    order = [lax.rem(ha // per + 1 + turn, CHUNKS) for turn in range(CHUNKS)]
+
+    def pick(h, _):
+        give[h] = acc[pl.ds((cores * h + mate) * share, tall)]
+        return 0
+
+    for chunk in order:
+        lax.fori_loop(chunk * per, chunk * per + per, pick, 0)
         pair(chunk).start()
 
-    for chunk in range(CHUNKS):
+    def scatter(s, chunk):
+        h = chunk * per + lax.rem(ha + s, per)
+
+        @pl.when(h != ha)
+        def _():
+            mine = acc[pl.ds((cores * h + ta) * share, tall)] + got[h]
+            out[h] = mine.astype(out.dtype)
+            spread(h, ha).start()
+
+        return chunk
+
+    for chunk in order:
         pair(chunk).wait_recv()
-
-    def scatter(s, _):
-        h = lax.rem(ha + s, rows)
-        mine = acc[pl.ds((cores * h + ta) * share, tall)] + got[h]
-        out[h] = mine.astype(out.dtype)
-        spread(h, ha).start()
-        return 0
-
-    lax.fori_loop(1, rows, scatter, 0)
+        lax.fori_loop(0, per, scatter, chunk)
+
+    for e in range(frames):
+        outer_input(e)
+
+    @pl.when(ta == 0)
+    def _():
+        for frame in range(2):
+            outer_input(frames + frame)
 
     def finish(t, _):
         summed = (
@@ -248,17 +313,18 @@
     for chunk in range(CHUNKS):
         pair(chunk).wait_send()
     for frame in range(frames):
-        for side in range(2):
-            @pl.when(sends[side])
-            def _():
-                halo(side, frame).wait_send()
+        near(frame, far_side).wait_send()
+
+        @pl.when(hands_on)
+        def _():
+            far(frame).wait_send()
 
     @pl.when(ta == 1)
     def _():
         for frame in range(2):
             ahead(frame).wait_send()
-            for side in range(2):
-                relay(side, frame).wait_send()
+            relay(near_side, 0, frame).wait_send()
+            relay(far_side, 1, frame).wait_send()
 
 
 def body(features, cotangent, kernel):
@@ -277,9 +343,13 @@
             jax.ShapeDtypeStruct((frames, breadth, channels), jnp.bfloat16),
             jax.ShapeDtypeStruct((share, channels), jnp.float32),
         ),
-        in_specs=[vmem] * 3,
+        in_specs=[pl.BlockSpec(memory_space=pltpu.HBM)] * 3,
         out_specs=(vmem, vmem),
         scratch_shapes=[
+            pltpu.VMEM((frames, breadth, channels), jnp.bfloat16),
+            pltpu.VMEM((frames, breadth, channels), jnp.bfloat16),
+            pltpu.VMEM((9, wide, channels), jnp.bfloat16),
+            dma((3,)),
             pltpu.VMEM((2, frames + 2, breadth, channels), jnp.bfloat16),
             pltpu.VMEM((2, breadth, channels), jnp.bfloat16),
             pltpu.VMEM((frames, breadth, wide), jnp.bfloat16),
@@ -290,7 +360,7 @@
             pltpu.VMEM((rows, tall, channels), jnp.float32),
             pltpu.VMEM((rows, tall, channels), jnp.bfloat16),
             pltpu.VMEM((rows, tall, channels), jnp.bfloat16),
-            dma((2, frames)), dma((2, frames)), dma((2,)), dma((2,)), dma((2, 2)), dma((2, 2)),
+            dma((frames,)), dma((frames,)), dma((frames,)), dma((frames,)), dma((2,)), dma((2,)), dma((2, 2)), dma((2, 2)),
             dma((CHUNKS,)), dma((CHUNKS,)), dma((rows,)), dma((rows,)),
         ],
         compiler_params=pltpu.CompilerParams(

time: 55.9 us -> 46.1 us (0.82)
  the two profiles are of different devices: /device:TPU:29 before, /device:TPU:0 now
where the time goes in v3:
time: 46.1 us; the launch traced here: 45.6 us
  Pallas kernels  40.2 us (87%)
  local copies, waits for them, and re-layouts  4.8 us (10%)
  between operations  0.65 us (1%)
    pallas_call x1, Pallas kernels, body(): pl.pallas_call(functools.partial(fused, rows, cores, factor), out_shape=(...  40.2 us
    unnamed x8, local copies, waits for them, and re-layouts  4.8 us

profile of v3, /device:TPU:0, one launch (start us, length us, event | category | flops | bytes accessed | tf_op | source)
XLA Modules:
  0.0 45.6 jit_solution(1818915879792739632)
XLA Ops:
  0.6 0.0 copy-start
  0.6 1.2 %copy-done = bf16[3,3,3,128,128]{4,3,2,1,0:T(8,128)(2,1)S(1)} copy-done((bf16[3,3,3,128,128]{4,3,2,1,0:T(8,128)(2,1)S(1)}, bf16[3,3,3,128,128]{4,3,2,1,0:T(8,128)(2,1)}, u32[]{:S(2)}) %copy-start) | copy-done | bytes 884760
  1.8 0.0 copy-start.1
  1.8 1.1 %copy-done.1 = bf16[4,1,640,128]{3,2,1,0:T(8,128)(2,1)S(1)} copy-done((bf16[4,1,640,128]{3,2,1,0:T(8,128)(2,1)S(1)}, bf16[4,1,640,128]{3,2,1,0:T(8,128)(2,1)}, u32[]{:S(2)}) %copy-start.1) | copy-done | bytes 655384
  2.9 0.0 copy-start.2
  2.9 1.1 %copy-done.2 = bf16[4,1,640,128]{3,2,1,0:T(8,128)(2,1)S(1)} copy-done((bf16[4,1,640,128]{3,2,1,0:T(8,128)(2,1)S(1)}, bf16[4,1,640,128]{3,2,1,0:T(8,128)(2,1)}, u32[]{:S(2)}) %copy-start.2) | copy-done | bytes 655384
  4.0 40.2 %shard_map.50 = (bf16[4,640,128]{2,1,0:T(8,128)(2,1)S(1)}, f32[108,128]{1,0:T(8,128)S(1)}) custom-call(bf16[4,640,128]{2,1,0:T(8,128)(2,1)S(1)} %bitcast.8, bf16[4,640,128]{2,1,0:T(8,128)(2,1)S(1)} %bitcast.9, bf16[9,384,128]{2,1,0:T(8,128)(2,1)S(1)} %bitcast.7), custom_call_target="tpu_custom_call" | custom-call | flops 4529848320 | bytes 2850816 | tf_op jit(solution)/shard_map/pallas_call | solution.py:340
  44.1 0.8 %copy.8 = bf16[4,1,640,128]{3,2,1,0:T(8,128)(2,1)} copy(bf16[4,1,640,128]{3,2,1,0:T(8,128)(2,1)S(1)} %bitcast.6) | data formatting | bytes 1310720
  45.0 0.6 %copy.9 = f32[108,128]{1,0:T(8,128)} copy(f32[108,128]{1,0:T(8,128)S(1)} %get-tuple-element.11) | data formatting | bytes 110592
Async XLA Ops:
  0.6 1.2 %copy-start = (bf16[3,3,3,128,128]{4,3,2,1,0:T(8,128)(2,1)S(1)}, bf16[3,3,3,128,128]{4,3,2,1,0:T(8,128)(2,1)}, u32[]{:S(2)}) copy-start(bf16[3,3,3,128,128]{4,3,2,1,0:T(8,128)(2,1)} %param.5) | copy-start | bytes 2654212
  1.8 1.1 %copy-start.1 = (bf16[4,1,640,128]{3,2,1,0:T(8,128)(2,1)S(1)}, bf16[4,1,640,128]{3,2,1,0:T(8,128)(2,1)}, u32[]{:S(2)}) copy-start(bf16[4,1,640,128]{3,2,1,0:T(8,128)(2,1)} %param.3) | copy-start | bytes 1966084
  2.9 1.1 %copy-start.2 = (bf16[4,1,640,128]{3,2,1,0:T(8,128)(2,1)S(1)}, bf16[4,1,640,128]{3,2,1,0:T(8,128)(2,1)}, u32[]{:S(2)}) copy-start(bf16[4,1,640,128]{3,2,1,0:T(8,128)(2,1)} %param.4) | copy-start | bytes 1966084

commit v4 on v3

--- a/solution.py
+++ b/solution.py
@@ -10,6 +10,7 @@
 MESH = pl.DeviceIdType.MESH
 LEAD = 8
 CHUNKS = 4
+HALVES = 2
 
 
 def fused(
@@ -45,22 +46,24 @@
     odd = lax.rem(ha, 2)
     near_side, far_side = 1 - odd, odd
 
-    def near(frame, side):
-        return pltpu.make_async_remote_copy(
-            src_ref=cot_hbm.at[frame],
-            dst_ref=ext.at[side, frame],
-            send_sem=near_send.at[frame],
-            recv_sem=near_recv.at[frame],
+    def near(piece, side):
+        frame, part = piece // HALVES, pl.ds(piece % HALVES * (breadth // HALVES), breadth // HALVES)
+        return pltpu.make_async_remote_copy(
+            src_ref=cot_hbm.at[frame, part],
+            dst_ref=ext.at[side, frame, part],
+            send_sem=near_send.at[piece],
+            recv_sem=near_recv.at[piece],
             device_id=(ha + 1 - 2 * odd, ta),
             device_id_type=MESH,
         )
 
-    def far(frame):
-        return pltpu.make_async_remote_copy(
-            src_ref=ext.at[near_side, frame],
-            dst_ref=ext.at[far_side, frame],
-            send_sem=far_send.at[frame],
-            recv_sem=far_recv.at[frame],
+    def far(piece):
+        frame, part = piece // HALVES, pl.ds(piece % HALVES * (breadth // HALVES), breadth // HALVES)
+        return pltpu.make_async_remote_copy(
+            src_ref=ext.at[near_side, frame, part],
+            dst_ref=ext.at[far_side, frame, part],
+            send_sem=far_send.at[piece],
+            recv_sem=far_recv.at[piece],
             device_id=(ha + 2 - 4 * odd, ta),
             device_id_type=MESH,
         )
@@ -90,8 +93,8 @@
     hands_on = jnp.logical_not(jnp.logical_or(jnp.logical_and(even, last), jnp.logical_and(odd == 1, first)))
     takes = jnp.logical_not(jnp.logical_or(jnp.logical_and(even, first), jnp.logical_and(odd == 1, last)))
 
-    for frame in range(frames):
-        near(frame, far_side).start()
+    for piece in range(frames * HALVES):
+        near(piece, far_side).start()
 
     @pl.when(ta == 1)
     def _():
@@ -106,7 +109,6 @@
     padded[:LEAD] = edge
     padded[LEAD + breadth :] = edge
     acc[...] = jnp.zeros_like(acc)
-    loads[0].wait()
 
     def activate(t, _):
         v = feat[t].astype(jnp.float32)
@@ -119,7 +121,6 @@
         partial[t] = jnp.zeros(partial.shape[1:], jnp.float32)
         return 0
 
-    lax.fori_loop(0, frames, activate, 0)
 
     nt = (((1,), (1,)), ((), ()))
     tn = (((0,), (0,)), ((), ()))
@@ -175,33 +176,41 @@
         def _():
             far(e).start()
 
-        if e < 2:
+        if e % HALVES == HALVES - 1 and e // HALVES < 2:
             @pl.when(ta == 1)
             def _():
-                relay(near_side, 0, e).start()
+                relay(near_side, 0, e // HALVES).start()
 
     def arrive(e):
         @pl.when(takes)
         def _():
-            far(e).wait_recv()
+            for part in range(HALVES):
+                far(e * HALVES + part).wait_recv()
 
         if e < 2:
             @pl.when(ta == 1)
             def _():
                 relay(far_side, 1, e).start()
 
+    loads[0].wait()
+    hand_on(0)
+    lax.fori_loop(0, 2, activate, 0)
+    hand_on(1)
+    lax.fori_loop(2, frames, activate, 0)
     loads[1].wait()
     loads[2].wait()
-    hand_on(0)
+    hand_on(2)
     middle(0, cot.at[0])
+    hand_on(3)
     middle(1, cot.at[1])
-    hand_on(1)
+    hand_on(4)
     middle(2, cot.at[2])
-    hand_on(2)
+    hand_on(5)
     arrive(0)
     outer_kernel(0)
+    hand_on(6)
     middle(3, cot.at[3])
-    hand_on(3)
+    hand_on(7)
     arrive(1)
     outer_kernel(1)
 
@@ -312,12 +321,12 @@
     lax.fori_loop(1, rows, drain, 0)
     for chunk in range(CHUNKS):
         pair(chunk).wait_send()
-    for frame in range(frames):
-        near(frame, far_side).wait_send()
+    for piece in range(frames * HALVES):
+        near(piece, far_side).wait_send()
 
         @pl.when(hands_on)
         def _():
-            far(frame).wait_send()
+            far(piece).wait_send()
 
     @pl.when(ta == 1)
     def _():
@@ -340,8 +349,8 @@
     grad_features, grad_kernel = pl.pallas_call(
         functools.partial(fused, rows, cores, factor),
         out_shape=(
-            jax.ShapeDtypeStruct((frames, breadth, channels), jnp.bfloat16),
-            jax.ShapeDtypeStruct((share, channels), jnp.float32),
+            pltpu.VMEM((frames, breadth, channels), jnp.bfloat16),
+            pltpu.VMEM((share, channels), jnp.float32),
         ),
         in_specs=[pl.BlockSpec(memory_space=pltpu.HBM)] * 3,
         out_specs=(vmem, vmem),
@@ -360,11 +369,11 @@
             pltpu.VMEM((rows, tall, channels), jnp.float32),
             pltpu.VMEM((rows, tall, channels), jnp.bfloat16),
             pltpu.VMEM((rows, tall, channels), jnp.bfloat16),
-            dma((frames,)), dma((frames,)), dma((frames,)), dma((frames,)), dma((2,)), dma((2,)), dma((2, 2)), dma((2, 2)),
+            dma((frames * HALVES,)), dma((frames * HALVES,)), dma((frames * HALVES,)), dma((frames * HALVES,)), dma((2,)), dma((2,)), dma((2, 2)), dma((2, 2)),
             dma((CHUNKS,)), dma((CHUNKS,)), dma((rows,)), dma((rows,)),
         ],
         compiler_params=pltpu.CompilerParams(
-            collective_id=0, has_side_effects=True, vmem_limit_bytes=48 * 1024 * 1024
+            collective_id=0, has_side_effects=True, vmem_limit_bytes=63 * 1024 * 1024
         ),
         cost_estimate=pl.CostEstimate(
             flops=4 * frames * breadth * taps * channels * channels,

time: 46.1 us -> 42.2 us (0.915)
  local copies, waits for them, and re-layouts: 4.8 us -> 1.46 us
  Pallas kernels: 40.2 us -> 39.7 us
    unnamed x8 -> x2, local copies, waits for them, and re-layouts: 4.8 us -> 1.46 us
    pallas_call x1, Pallas kernels: 40.2 us -> 39.7 us  [body(): pl.pallas_call(functools.partial(fused, rows, cores, factor), out_shape=(...]
where the time goes in v4:
time: 42.2 us; the launch traced here: 41.8 us
  Pallas kernels  39.7 us (94%)
  local copies, waits for them, and re-layouts  1.46 us (3%)
  between operations  0.64 us (2%)
    pallas_call x1, Pallas kernels, body(): pl.pallas_call(functools.partial(fused, rows, cores, factor), out_shape=(...  39.7 us
    unnamed x2, local copies, waits for them, and re-layouts  1.46 us

profile of v4, /device:TPU:0, one launch (start us, length us, event | category | flops | bytes accessed | tf_op | source)
XLA Modules:
  0.0 41.8 jit_solution(16234660129207215842)
XLA Ops:
  0.6 39.7 %shard_map.50 = (bf16[4,640,128]{2,1,0:T(8,128)(2,1)S(1)}, f32[108,128]{1,0:T(8,128)S(1)}) custom-call(bf16[4,640,128]{2,1,0:T(8,128)(2,1)} %bitcast.8, bf16[4,640,128]{2,1,0:T(8,128)(2,1)} %bitcast.9, bf16[9,384,128]{2,1,0:T(8,128)(2,1)} %bitcast.7), custom_call_target="tpu_custom_call" | custom-call | flops 4529848320 | bytes 2850816 | tf_op jit(solution)/shard_map/pallas_call | solution.py:349
  40.3 0.8 %copy.8 = bf16[4,1,640,128]{3,2,1,0:T(8,128)(2,1)} copy(bf16[4,1,640,128]{3,2,1,0:T(8,128)(2,1)S(1)} %bitcast.6) | data formatting | bytes 1310720
  41.2 0.6 %copy.9 = f32[108,128]{1,0:T(8,128)} copy(f32[108,128]{1,0:T(8,128)S(1)} %get-tuple-element.9) | data formatting | bytes 110592

commit v5 on v4

--- a/solution.py
+++ b/solution.py
@@ -259,7 +259,7 @@
     order = [lax.rem(ha // per + 1 + turn, CHUNKS) for turn in range(CHUNKS)]
 
     def pick(h, _):
-        give[h] = acc[pl.ds((cores * h + mate) * share, tall)]
+        give[h] = acc[pl.ds((cores * h + mate) * share, tall)].astype(give.dtype)
         return 0
 
     for chunk in order:
@@ -271,7 +271,7 @@
 
         @pl.when(h != ha)
         def _():
-            mine = acc[pl.ds((cores * h + ta) * share, tall)] + got[h]
+            mine = acc[pl.ds((cores * h + ta) * share, tall)] + got[h].astype(jnp.float32)
             out[h] = mine.astype(out.dtype)
             spread(h, ha).start()
 
@@ -303,7 +303,7 @@
 
     lax.fori_loop(0, frames, finish, 0)
 
-    total = acc[pl.ds((cores * ha + ta) * share, tall)] + got[ha]
+    total = acc[pl.ds((cores * ha + ta) * share, tall)] + got[ha].astype(jnp.float32)
 
     def collect(s, total):
         h = lax.rem(ha + rows - s, rows)
@@ -365,8 +365,8 @@
             pltpu.VMEM((breadth + 2 * LEAD, channels), jnp.float32),
             pltpu.VMEM((frames, breadth + 2 * LEAD, wide), jnp.float32),
             pltpu.VMEM((taps * channels + 16, channels), jnp.float32),
-            pltpu.VMEM((rows, tall, channels), jnp.float32),
-            pltpu.VMEM((rows, tall, channels), jnp.float32),
+            pltpu.VMEM((rows, tall, channels), jnp.bfloat16),
+            pltpu.VMEM((rows, tall, channels), jnp.bfloat16),
             pltpu.VMEM((rows, tall, channels), jnp.bfloat16),
             pltpu.VMEM((rows, tall, channels), jnp.bfloat16),
             dma((frames * HALVES,)), dma((frames * HALVES,)), dma((frames * HALVES,)), dma((frames * HALVES,)), dma((2,)), dma((2,)), dma((2, 2)), dma((2, 2)),

time: 42.2 us -> 42.2 us (level)
  no operation moved by 1% of the time
where the time goes in v5:
time: 42.2 us; the launch traced here: 41.8 us
  Pallas kernels  39.7 us (94%)
  local copies, waits for them, and re-layouts  1.46 us (3%)
  between operations  0.64 us (2%)
    pallas_call x1, Pallas kernels, body(): pl.pallas_call(functools.partial(fused, rows, cores, factor), out_shape=(...  39.7 us
    unnamed x2, local copies, waits for them, and re-layouts  1.46 us

profile of v5, /device:TPU:0, one launch (start us, length us, event | category | flops | bytes accessed | tf_op | source)
XLA Modules:
  0.0 41.8 jit_solution(2458926551979042563)
XLA Ops:
  0.6 39.7 %shard_map.50 = (bf16[4,640,128]{2,1,0:T(8,128)(2,1)S(1)}, f32[108,128]{1,0:T(8,128)S(1)}) custom-call(bf16[4,640,128]{2,1,0:T(8,128)(2,1)} %bitcast.8, bf16[4,640,128]{2,1,0:T(8,128)(2,1)} %bitcast.9, bf16[9,384,128]{2,1,0:T(8,128)(2,1)} %bitcast.7), custom_call_target="tpu_custom_call" | custom-call | flops 4529848320 | bytes 2850816 | tf_op jit(solution)/shard_map/pallas_call | solution.py:349
  40.4 0.8 %copy.8 = bf16[4,1,640,128]{3,2,1,0:T(8,128)(2,1)} copy(bf16[4,1,640,128]{3,2,1,0:T(8,128)(2,1)S(1)} %bitcast.6) | data formatting | bytes 1310720
  41.2 0.6 %copy.9 = f32[108,128]{1,0:T(8,128)} copy(f32[108,128]{1,0:T(8,128)S(1)} %get-tuple-element.9) | data formatting | bytes 110592
